TPU v7x, 32 devices: a whole 2x2x4 slice. The times are simulated.
32 devices in a mesh: group: 2 (over y), graph: 4 (over z), member: 4 (over x, core).
Axes of the slice: x: 2, y: 2, z: 4, core: 2. Of those that a mesh axis runs over, the one named last changes fastest.
Arguments:
- fine_nodes: bfloat16 [8, 1024, 512], P(('group', 'member'), 'graph'), parts along dimension 0, may hold values from -6 to 6
- coarse_nodes: bfloat16 [8, 80, 512], P(('group', 'member')), parts along dimension 0, may hold values from -6 to 6
- edge_latents: bfloat16 [8, 3072, 512], P(('group', 'member'), 'graph'), parts along dimension 0, may hold values from -6 to 6
- edge_send: int32 [3072], P('graph'), may hold values from 0 to 367, as said below
- edge_recv: int32 [3072], P('graph'), may hold values from 0 to 367, as said below
- edge_count: int32 [4], P('graph'), may hold values from 192 to 768, as said below
- send_index: int32 [4, 4, 8], P('graph'), may hold values from 0 to 255, as said below
- send_count: int32 [4, 4], P('graph'), may hold values from 0 to 8, as said below
- edge_w1: bfloat16 [2, 1536, 512], P(None, 'graph'), may hold values from -0.15625 to 0.15625
- edge_w2: bfloat16 [2, 512, 512], P(None, 'graph'), may hold values from -0.25 to 0.25
- node_w1: bfloat16 [2, 1024, 512], P(None, 'graph'), may hold values from -0.1875 to 0.1875
- node_w2: bfloat16 [2, 512, 512], P(None, 'graph'), may hold values from -0.25 to 0.25
- edge_bias: float32 [2, 512], replicated, may hold values from -3 to 3
- edge_gain: float32 [2, 512], replicated, may hold values from 0.1 to 1.9
- node_bias: float32 [2, 512], replicated, may hold values from -3 to 3
- node_gain: float32 [2, 512], replicated, may hold values from 0.1 to 1.9
Outputs:
- fine_out: bfloat16 [8, 1024, 512], P(('group', 'member'), 'graph'), parts along dimension 0
- coarse_out: bfloat16 [8, 80, 512], P(('group', 'member')), parts along dimension 0
- edge_out: bfloat16 [8, 3072, 512], P(('group', 'member'), 'graph'), parts along dimension 0
There are 2 independent parts, one for each index of `group`. A program takes and returns all parts, laid end to end along the dimension named above; an argument that names none is the same for every part. Nothing has to cross between parts.
Inputs may be any that keep to these rules, and one draw needn't show every extreme that they name: `edge_send`: A local index below 368; it never names a slot s of the list from p at or past send_count[p, g]. `edge_recv`: as for edge_send. `edge_count`: some index of graph has all its edge slots live. `send_index`: slots at or past the count hold 0. send_count[p, p] = 0; the list from p to (p + 1) mod 4 is full.
All inputs are finite; a program needn't handle non-finite values.
Results may differ from a plain program's by a relative error of at most 0.0085.
Values may be sent and summed in bfloat16 or wider, within the bound.
A program may use at most 64 MiB of HBM per device.

v0:
```python
import jax
import jax.numpy as jnp
from jax import lax
from jax.sharding import PartitionSpec as P


def layer_norm(projected, gain_row):
    average = jnp.mean(projected, axis=-1, keepdims=True)
    centered = projected - average
    variance = jnp.mean(centered * centered, axis=-1, keepdims=True)
    return centered * lax.rsqrt(variance + 1e-05) * gain_row


def project(inputs, weight):
    full_weight = lax.all_gather(weight, "graph", axis=0, tiled=True)
    return jnp.dot(inputs, full_weight, preferred_element_type=jnp.float32)


def two_layer(inputs, first_weight, bias_row, second_weight, gain_row):
    hidden = jax.nn.silu(project(inputs, first_weight) + bias_row).astype(jnp.bfloat16)
    return layer_norm(project(hidden, second_weight), gain_row)


def scatter_rows(values, indices, count):
    return jax.vmap(
        lambda member_rows: jax.ops.segment_sum(member_rows, indices, num_segments=count)
    )(values)


def node_step(states, sum_rows, first_weight, bias_row, second_weight, gain_row):
    members, row_count, latent = states.shape
    inputs = jnp.concatenate([states, sum_rows.astype(jnp.bfloat16)], axis=2).reshape(
        members * row_count, 2 * latent
    )
    change = two_layer(inputs, first_weight, bias_row, second_weight, gain_row).reshape(
        members, row_count, latent
    )
    return (states.astype(jnp.float32) + change).astype(jnp.bfloat16)


def on_device(
    fine_nodes,
    coarse_nodes,
    edge_latents,
    edge_send,
    edge_recv,
    edge_count,
    send_index,
    send_count,
    edge_w1,
    edge_w2,
    node_w1,
    node_w2,
    edge_bias,
    edge_gain,
    node_bias,
    node_gain,
):
    peer_count = lax.axis_size("graph")
    members, owned_rows, latent = fine_nodes.shape
    slot_count = send_index.shape[2]
    coarse_total = coarse_nodes.shape[1]
    edge_slots = edge_latents.shape[1]
    mirror_base = coarse_total + owned_rows
    table_rows = mirror_base + peer_count * slot_count
    live_edge = jnp.arange(edge_slots, dtype=jnp.int32) < edge_count[0]
    send_lists = send_index[0].reshape(peer_count * slot_count)
    used_out = jnp.arange(slot_count, dtype=jnp.int32)[None, :] < send_count[0][:, None]
    counts_out = send_count.reshape(1, peer_count, 1)
    zero_row = jnp.zeros((), jnp.bfloat16)
    fine_state = fine_nodes
    coarse_state = coarse_nodes
    edge_state = edge_latents
    for layer_idx in range(edge_w1.shape[0]):
        outgoing = fine_state[:, send_lists].reshape(members, peer_count, slot_count, latent)
        incoming, counts_in = (
            lax.all_to_all(outgoing, "graph", split_axis=1, concat_axis=1, tiled=True),
            lax.all_to_all(counts_out, "graph", split_axis=1, concat_axis=1, tiled=True),
        )
        used_in = (
            jnp.arange(slot_count, dtype=jnp.int32)[None, :]
            < counts_in.reshape(peer_count)[:, None]
        )
        mirrors = jnp.where(used_in[None, :, :, None], incoming, zero_row).reshape(
            members, peer_count * slot_count, latent
        )
        node_table = jnp.concatenate([coarse_state, fine_state, mirrors], axis=1)
        table_ok = jnp.concatenate(
            [jnp.ones((mirror_base,), bool), used_in.reshape(peer_count * slot_count)]
        )
        senders = node_table[:, edge_send]
        receivers = node_table[:, edge_recv]
        inputs = jnp.concatenate([edge_state, senders, receivers], axis=2).reshape(
            members * edge_slots, 3 * latent
        )
        update = two_layer(
            inputs,
            edge_w1[layer_idx],
            edge_bias[layer_idx],
            edge_w2[layer_idx],
            edge_gain[layer_idx],
        )
        update = update.reshape(members, edge_slots, latent)
        edge_state = (
            edge_state.astype(jnp.float32)
            + jnp.where(live_edge[None, :, None], update, jnp.float32(0.0))
        ).astype(jnp.bfloat16)
        kept_edge = jnp.logical_and(live_edge, table_ok[edge_recv])
        messages = jnp.where(kept_edge[None, :, None], update, jnp.float32(0.0))
        totals = scatter_rows(messages, edge_recv, table_rows)
        coarse_part = totals[:, :coarse_total]
        own_part = totals[:, coarse_total:mirror_base]
        mirror_part = totals[:, mirror_base:].reshape(members, peer_count, slot_count, latent)
        returned = lax.all_to_all(mirror_part, "graph", split_axis=1, concat_axis=1, tiled=True)
        returned = jnp.where(used_out[None, :, :, None], returned, jnp.float32(0.0))
        own_part = own_part + scatter_rows(
            returned.reshape(members, peer_count * slot_count, latent), send_lists, owned_rows
        )
        coarse_sum = lax.psum(coarse_part, "graph")
        states = jnp.concatenate([coarse_state, fine_state], axis=1)
        sum_rows = jnp.concatenate([coarse_sum, own_part], axis=1)
        updated = node_step(
            states,
            sum_rows,
            node_w1[layer_idx],
            node_bias[layer_idx],
            node_w2[layer_idx],
            node_gain[layer_idx],
        )
        coarse_state = updated[:, :coarse_total]
        fine_state = updated[:, coarse_total:]
    return (fine_state, coarse_state, edge_state)


def solution(mesh):
    placed = (
        P(("group", "member"), "graph", None),
        P(("group", "member"), None, None),
        P(("group", "member"), "graph", None),
        P("graph"),
        P("graph"),
        P("graph"),
        P("graph", None, None),
        P("graph", None),
        P(None, "graph", None),
        P(None, "graph", None),
        P(None, "graph", None),
        P(None, "graph", None),
        P(),
        P(),
        P(),
        P(),
    )
    return jax.shard_map(
        on_device,
        mesh=mesh,
        in_specs=placed,
        out_specs=(
            P(("group", "member"), "graph", None),
            P(("group", "member"), None, None),
            P(("group", "member"), "graph", None),
        ),
        check_vma=False,
    )
```

profile of v0, /device:TPU:0, one launch (start us, length us, event | category | flops | bytes accessed | tf_op | source)
XLA Modules:
  0.0 243.2 jit_solution(18142849734779911968)
XLA Ops:
  7.2 2.1 fusion.89
  11.8 6.3 %all-to-all-start = ((s32[1,4,1]{2,0,1:T(1,128)}), s32[1,4,1]{2,0,1:T(1,128)S(1)}, u32[]{:S(2)}, u32[]{:S(2)}) async-start(s32[1,4,1]{2,0,1:T(1,128)} %copy.40), calls=%async_computation | async-start | bytes 4096 | tf_op jit(solution)/shard_map/all_to_all | solution.py:78
  19.4 23.5 %all-gather.1 = bf16[1,512,512]{2,1,0:T(8,128)(2,1)} all-gather(bf16[1,128,512]{2,1,0:T(8,128)(2,1)S(1)} %get-tuple-element.22), channel_id=3, replica_groups=mesh['group'=2,'graph'=4,'member'=4] {'graph'}, dimensions={1}, use_global_device_ids=true | all-gather | bytes 655360 | tf_op jit(solution)/shard_map/all_gather | solution.py:15
  44.3 22.1 %all-gather.3 = bf16[1,512,512]{2,1,0:T(8,128)(2,1)} all-gather(bf16[1,128,512]{2,1,0:T(8,128)(2,1)S(1)} %get-tuple-element.20), channel_id=5, replica_groups=mesh['group'=2,'graph'=4,'member'=4] {'graph'}, dimensions={1}, use_global_device_ids=true | all-gather | bytes 655360 | tf_op jit(solution)/shard_map/all_gather | solution.py:15
  68.7 20.2 %all-gather.5 = bf16[1,512,512]{2,1,0:T(8,128)(2,1)} all-gather(bf16[1,128,512]{2,1,0:T(8,128)(2,1)S(1)} %get-tuple-element.21), channel_id=7, replica_groups=mesh['group'=2,'graph'=4,'member'=4] {'graph'}, dimensions={1}, use_global_device_ids=true | all-gather | bytes 655360 | tf_op jit(solution)/shard_map/all_gather | solution.py:15
  88.9 20.2 %all-gather.7 = bf16[1,512,512]{2,1,0:T(8,128)(2,1)} all-gather(bf16[1,128,512]{2,1,0:T(8,128)(2,1)S(1)} %get-tuple-element.19), channel_id=9, replica_groups=mesh['group'=2,'graph'=4,'member'=4] {'graph'}, dimensions={1}, use_global_device_ids=true | all-gather | bytes 655360 | tf_op jit(solution)/shard_map/all_gather | solution.py:15
  110.3 3.3 %all-to-all-start.1 = ((bf16[1,4,8,512]{3,2,0,1:T(8,128)(2,1)}), bf16[1,4,8,512]{3,2,0,1:T(8,128)(2,1)S(1)}, u32[]{:S(2)}, u32[]{:S(2)}) async-start(bf16[1,4,8,512]{3,2,0,1:T(8,128)(2,1)} %bitcast.6), calls=%async_computation.1 | async-start | bytes 65536 | tf_op jit(solution)/shard_map/all_to_all | solution.py:77
  114.0 4.8 %gather_fusion = pred[768]{0:T(1024)(128)(4,1)S(1)} fusion(pred[368]{0:T(512)(128)(4,1)S(1)} %concatenate.62, s32[1024]{0:T(1024)S(1)} %pad_clamp_fusion.2), kind=kCustom, calls=%fused_computation | custom fusion | bytes 4608 | tf_op jit(solution)/shard_map/gather | solution.py:108
  119.5 2.7 %gather_fusion.3 = bf16[768,512]{1,0:T(8,128)(2,1)S(1)} fusion(bf16[368,512]{1,0:T(8,128)(2,1)S(1)} %maximum_bitcast_fusion.24, s32[1024]{0:T(1024)S(1)} %pad_clamp_fusion.2), kind=kCustom, calls=%fused_computation.3 | custom fusion | bytes 1575936 | tf_op jit(solution)/shard_map/gather | solution.py:92
  122.2 2.7 %gather_fusion.2 = bf16[768,512]{1,0:T(8,128)(2,1)S(1)} fusion(bf16[368,512]{1,0:T(8,128)(2,1)S(1)} %maximum_bitcast_fusion.24, s32[1024]{0:T(1024)S(1)} %pad_clamp_fusion), kind=kCustom, calls=%fused_computation.2 | custom fusion | bytes 1575936 | tf_op jit(solution)/shard_map/gather | solution.py:91
  124.9 3.6 %fusion.97 = (f32[768]{0:T(1024)S(1)}, f32[768,512]{0,1:T(8,128)S(1)}) fusion(bf16[1,512,512]{2,1,0:T(8,128)(2,1)} %all-gather.1, bf16[1,1536,512]{2,1,0:T(8,128)(2,1)} %all-gather.13.cloned.1.call-done, bf16[1,768,512]{2,1,0:T(8,128)(2,1)S(1)} %bitcast.175, bf16[1,768,512]{2,1,0:T(8,128)(2,1)S(1)} %bitcast.176, bf16[1,768,512]{2,1,0:T(8,128)(2,1)} %param.18, ...), kind=kOutput, calls=%fused_computation.136 | convolution fusion | flops 1620442368 | bytes 6034432 | tf_op jit(solution)/shard_map/dot_general | solution.py:16
  130.6 7.4 %scatter_custom_fusion = f32[368,512]{1,0:T(8,128)S(1)} fusion(s32[768]{0:T(1024)S(1)} %copy-done.18, f32[768,512]{1,0:T(8,128)} %copy.42, f32[]{:T(128)} %constant.12.clone.1), kind=kCustom, calls=%fused_computation.77 | custom fusion | flops 393216 | bytes 754176 | tf_op jit(solution)/shard_map/vmap()/scatter-add | solution.py:26
  138.8 4.5 %all-to-all-start.2 = ((f32[1,4,8,512]{3,2,0,1:T(8,128)}), f32[1,4,8,512]{3,2,0,1:T(8,128)S(1)}, u32[]{:S(2)}, u32[]{:S(2)}) async-start(f32[1,4,8,512]{3,2,0,1:T(8,128)} %slice_bitcast_fusion.4), calls=%async_computation.2 | async-start | bytes 131072 | tf_op jit(solution)/shard_map/all_to_all | solution.py:114
  143.2 24.4 %all-reduce.3 = bf16[1,80,512]{2,1,0:T(8,128)(2,1)S(1)} all-reduce(f32[1,80,512]{2,1,0:T(8,128)S(1)} %slice.117), channel_id=1, replica_groups=mesh['group'=2,'graph'=4,'member'=4] {'graph'}, use_global_device_ids=true, to_apply=%region_3.4 | all-reduce | flops 40960 | bytes 245760 | tf_op jit(solution)/shard_map/psum | solution.py:119
  169.0 2.3 fusion.100
  174.0 3.4 %all-to-all-start.3 = ((bf16[1,4,8,512]{3,2,0,1:T(8,128)(2,1)}), bf16[1,4,8,512]{3,2,0,1:T(8,128)(2,1)S(1)}, u32[]{:S(2)}, u32[]{:S(2)}) async-start(bf16[1,4,8,512]{3,2,0,1:T(8,128)(2,1)} %bitcast.32), calls=%async_computation.3 | async-start | bytes 65536 | tf_op jit(solution)/shard_map/all_to_all | solution.py:77
  178.5 4.5 %all-to-all-done.3 = bf16[1,4,8,512]{3,2,0,1:T(8,128)(2,1)S(1)} async-done(((bf16[1,4,8,512]{3,2,0,1:T(8,128)(2,1)}), bf16[1,4,8,512]{3,2,0,1:T(8,128)(2,1)S(1)}, u32[]{:S(2)}, u32[]{:S(2)}) %all-to-all-start.3) | async-done | bytes 32800 | tf_op jit(solution)/shard_map/all_to_all | solution.py:77
  183.6 2.7 %gather_fusion.5 = bf16[768,512]{1,0:T(8,128)(2,1)S(1)} fusion(bf16[368,512]{1,0:T(8,128)(2,1)S(1)} %maximum_bitcast_fusion.25, s32[1024]{0:T(1024)S(1)} %pad_clamp_fusion), kind=kCustom, calls=%fused_computation.5 | custom fusion | bytes 1575936 | tf_op jit(solution)/shard_map/gather | solution.py:91
  186.3 2.7 %gather_fusion.6 = bf16[768,512]{1,0:T(8,128)(2,1)S(1)} fusion(bf16[368,512]{1,0:T(8,128)(2,1)S(1)} %maximum_bitcast_fusion.25, s32[1024]{0:T(1024)S(1)} %pad_clamp_fusion.2), kind=kCustom, calls=%fused_computation.6 | custom fusion | bytes 1575936 | tf_op jit(solution)/shard_map/gather | solution.py:92
  190.4 3.6 %fusion.103 = (f32[768]{0:T(1024)S(1)}, f32[768,512]{0,1:T(8,128)S(1)}) fusion(bf16[1,512,512]{2,1,0:T(8,128)(2,1)} %all-gather.5, bf16[1,1536,512]{2,1,0:T(8,128)(2,1)} %all-gather.17.cloned.1.call-done, bf16[1,768,512]{1,2,0:T(8,128)(2,1)} %bitcast.178, bf16[1,768,512]{1,2,0:T(8,128)(2,1)S(1)} %bitcast.177, bf16[1,768,512]{1,2,0:T(8,128)(2,1)S(1)} %fusion.12, ...), kind=kOutput, calls=%fused_computation.138 | convolution fusion | flops 1620442368 | bytes 6034432 | tf_op jit(solution)/shard_map/dot_general | solution.py:16
  198.1 7.4 %scatter_custom_fusion.2 = f32[368,512]{1,0:T(8,128)S(1)} fusion(s32[768]{0:T(1024)} %param.20, f32[768,512]{1,0:T(8,128)} %copy.48, f32[]{:T(128)} %constant.12.clone.1), kind=kCustom, calls=%fused_computation.75 | custom fusion | flops 393216 | bytes 754176 | tf_op jit(solution)/shard_map/vmap()/scatter-add | solution.py:26
  206.2 3.3 %all-to-all-start.4 = ((f32[1,4,8,512]{3,2,0,1:T(8,128)}), f32[1,4,8,512]{3,2,0,1:T(8,128)S(1)}, u32[]{:S(2)}, u32[]{:S(2)}) async-start(f32[1,4,8,512]{3,2,0,1:T(8,128)} %slice_bitcast_fusion.3), calls=%async_computation.4 | async-start | bytes 131072 | tf_op jit(solution)/shard_map/all_to_all | solution.py:114
  209.5 21.8 %all-reduce.4 = bf16[1,80,512]{2,1,0:T(8,128)(2,1)S(1)} all-reduce(f32[1,80,512]{2,1,0:T(8,128)S(1)} %slice.121), channel_id=1, replica_groups=mesh['group'=2,'graph'=4,'member'=4] {'graph'}, use_global_device_ids=true, to_apply=%region_10.11 | all-reduce | flops 40960 | bytes 245760 | tf_op jit(solution)/shard_map/psum | solution.py:119
  232.6 2.2 fusion.106
  (132 shorter events, 26.6 us)
Async XLA Ops:
  7.2 117.7 %all-gather.13.cloned.1.call-start = ((), (), s32[]{:S(2)}) async-start(), calls=%async_computation.5 | async-start | bytes 1966080 | tf_op jit(solution)/shard_map/all_gather | solution.py:15
  9.3 10.1 %copy-start.9 = (bf16[2,128,512]{2,1,0:T(8,128)(2,1)S(1)}, bf16[2,128,512]{2,1,0:T(8,128)(2,1)}, u32[]{:S(2)}) copy-start(bf16[2,128,512]{2,1,0:T(8,128)(2,1)} %param.25) | copy-start | bytes 786436
  9.4 33.6 %copy-start.14 = (f32[2,512]{1,0:T(2,128)S(1)}, f32[2,512]{1,0:T(2,128)}, u32[]{:S(2)}) copy-start(f32[2,512]{1,0:T(2,128)} %param.28) | copy-start | bytes 12292
  9.4 34.8 %copy-start.15 = (f32[2,512]{1,0:T(2,128)S(1)}, f32[2,512]{1,0:T(2,128)}, u32[]{:S(2)}) copy-start(f32[2,512]{1,0:T(2,128)} %param.29) | copy-start | bytes 12292
  9.4 34.9 %copy-start.10 = (bf16[2,128,512]{2,1,0:T(8,128)(2,1)S(1)}, bf16[2,128,512]{2,1,0:T(8,128)(2,1)}, u32[]{:S(2)}) copy-start(bf16[2,128,512]{2,1,0:T(8,128)(2,1)} %param.27) | copy-start | bytes 786436
  9.4 159.5 %all-gather.15.cloned.1.call-start = ((), (), s32[]{:S(2)}) async-start(), calls=%async_computation.6 | async-start | bytes 1310720 | tf_op jit(solution)/shard_map/all_gather | solution.py:15
  10.3 56.1 %copy-start.16 = (f32[2,512]{1,0:T(2,128)S(1)}, f32[2,512]{1,0:T(2,128)}, u32[]{:S(2)}) copy-start(f32[2,512]{1,0:T(2,128)} %param.30) | copy-start | bytes 12292
  10.3 56.7 %copy-start.17 = (f32[2,512]{1,0:T(2,128)S(1)}, f32[2,512]{1,0:T(2,128)}, u32[]{:S(2)}) copy-start(f32[2,512]{1,0:T(2,128)} %param.31) | copy-start | bytes 12292
  10.3 57.2 %copy-start.3 = (bf16[1,768,512]{2,1,0:T(8,128)(2,1)S(1)}, bf16[1,768,512]{2,1,0:T(8,128)(2,1)}, u32[]{:S(2)}) copy-start(bf16[1,768,512]{2,1,0:T(8,128)(2,1)} %param.18) | copy-start | bytes 2359300
  10.4 180.1 %all-gather.17.cloned.1.call-start = ((), (), s32[]{:S(2)}) async-start(), calls=%async_computation.7 | async-start | bytes 1966080 | tf_op jit(solution)/shard_map/all_gather | solution.py:15
  11.8 98.5 %all-to-all-start = ((s32[1,4,1]{2,0,1:T(1,128)}), s32[1,4,1]{2,0,1:T(1,128)S(1)}, u32[]{:S(2)}, u32[]{:S(2)}) async-start(s32[1,4,1]{2,0,1:T(1,128)} %copy.40), calls=%async_computation | async-start | bytes 4096 | tf_op jit(solution)/shard_map/all_to_all | solution.py:78
  18.1 214.5 %all-gather.19.cloned.1.call-start = ((), (), s32[]{:S(2)}) async-start(), calls=%async_computation.8 | async-start | bytes 1310720 | tf_op jit(solution)/shard_map/all_gather | solution.py:15
  44.3 123.4 %copy-start.19 = (pred[4,8]{1,0:T(4,128)(4,1)}, pred[4,8]{1,0:T(4,128)(4,1)S(1)}, u32[]{:S(2)}) copy-start(pred[4,8]{1,0:T(4,128)(4,1)S(1)} %iota_compare_fusion.1) | copy-start | bytes 100
  66.4 42.6 %copy-start.1 = (bf16[1,256,512]{2,1,0:T(8,128)(2,1)S(1)}, bf16[1,256,512]{2,1,0:T(8,128)(2,1)}, u32[]{:S(2)}) copy-start(bf16[1,256,512]{2,1,0:T(8,128)(2,1)} %param.16) | copy-start | bytes 786436
  68.7 50.8 %copy-start.6 = (bf16[1,80,512]{2,1,0:T(8,128)(2,1)S(1)}, bf16[1,80,512]{2,1,0:T(8,128)(2,1)}, u32[]{:S(2)}) copy-start(bf16[1,80,512]{2,1,0:T(8,128)(2,1)} %param.17) | copy-start | bytes 245764
  110.3 9.1 %all-to-all-start.1 = ((bf16[1,4,8,512]{3,2,0,1:T(8,128)(2,1)}), bf16[1,4,8,512]{3,2,0,1:T(8,128)(2,1)S(1)}, u32[]{:S(2)}, u32[]{:S(2)}) async-start(bf16[1,4,8,512]{3,2,0,1:T(8,128)(2,1)} %bitcast.6), calls=%async_computation.1 | async-start | bytes 65536 | tf_op jit(solution)/shard_map/all_to_all | solution.py:77
  138.0 30.9 %copy-start.2 = (bf16[1,256,512]{2,1,0:T(8,128)(2,1)S(1)}, bf16[1,256,512]{2,1,0:T(8,128)(2,1)}, u32[]{:S(2)}) copy-start(bf16[1,256,512]{2,1,0:T(8,128)(2,1)} %param.16) | copy-start | bytes 786436
  138.1 30.9 %copy-start.7 = (bf16[1,80,512]{2,1,0:T(8,128)(2,1)S(1)}, bf16[1,80,512]{2,1,0:T(8,128)(2,1)}, u32[]{:S(2)}) copy-start(bf16[1,80,512]{2,1,0:T(8,128)(2,1)} %param.17) | copy-start | bytes 245764
  138.8 28.9 %all-to-all-start.2 = ((f32[1,4,8,512]{3,2,0,1:T(8,128)}), f32[1,4,8,512]{3,2,0,1:T(8,128)S(1)}, u32[]{:S(2)}, u32[]{:S(2)}) async-start(f32[1,4,8,512]{3,2,0,1:T(8,128)} %slice_bitcast_fusion.4), calls=%async_computation.2 | async-start | bytes 131072 | tf_op jit(solution)/shard_map/all_to_all | solution.py:114
  174.0 8.9 %all-to-all-start.3 = ((bf16[1,4,8,512]{3,2,0,1:T(8,128)(2,1)}), bf16[1,4,8,512]{3,2,0,1:T(8,128)(2,1)S(1)}, u32[]{:S(2)}, u32[]{:S(2)}) async-start(bf16[1,4,8,512]{3,2,0,1:T(8,128)(2,1)} %bitcast.32), calls=%async_computation.3 | async-start | bytes 65536 | tf_op jit(solution)/shard_map/all_to_all | solution.py:77
  198.1 33.2 %copy-start.20 = (pred[4,8]{1,0:T(4,128)(4,1)S(1)}, pred[4,8]{1,0:T(4,128)(4,1)}, u32[]{:S(2)}) copy-start(pred[4,8]{1,0:T(4,128)(4,1)} %copy-done.19) | copy-start | bytes 100
  205.5 27.1 %copy-start.4 = (bf16[1,512,512]{2,1,0:T(8,128)(2,1)S(1)}, bf16[1,512,512]{2,1,0:T(8,128)(2,1)}, u32[]{:S(2)}) copy-start(bf16[1,512,512]{2,1,0:T(8,128)(2,1)} %all-gather.7) | copy-start | bytes 1572868
  205.5 27.1 %copy-start.22 = (f32[1,512]{1,0:T(1,128)S(1)}, f32[1,512]{1,0:T(1,128)}, u32[]{:S(2)}) copy-start(f32[1,512]{1,0:T(1,128)} %get-tuple-element.25) | copy-start | bytes 6148
  206.2 25.1 %all-to-all-start.4 = ((f32[1,4,8,512]{3,2,0,1:T(8,128)}), f32[1,4,8,512]{3,2,0,1:T(8,128)S(1)}, u32[]{:S(2)}, u32[]{:S(2)}) async-start(f32[1,4,8,512]{3,2,0,1:T(8,128)} %slice_bitcast_fusion.3), calls=%async_computation.4 | async-start | bytes 131072 | tf_op jit(solution)/shard_map/all_to_all | solution.py:114
  (10 other events, 54.8 us)
Sparse Core Ops, SparseCore 0:
  9.6 56.4 all-gather.12
  68.2 38.2 all-gather.14
  108.2 38.1 all-gather.16
  147.8 28.0 all-gather.18
where the time goes:
time: 244 us; the launch traced here: 243 us
  blocking collectives  132 us (54%)
  local copies, waits for them, and re-layouts  33.9 us (14%)
  other arithmetic  23.1 us (9%)
  starting transfers between devices  20.9 us (9%)
  between operations  15.1 us (6%)
  matrix products  11.7 us (5%)
  waiting for transfers between devices  6.42 us (3%)
    all_gather x4, blocking collectives, project(): full_weight = lax.all_gather(weight, 'graph', axis=0, tiled=True)  85.9 us
    psum x2, blocking collectives, on_device(): coarse_sum = lax.psum(coarse_part, 'graph')  46.2 us
    scatter-add x4, other arithmetic, scatter_rows(): jax.ops.segment_sum(member_rows, indices, num_segments=count)  17.3 us
    dot_general x4, matrix products, project(): return jnp.dot(inputs, full_weight, preferred_element_type=jnp.float32)  11.7 us
    all_to_all x2, starting transfers between devices, on_device(): lax.all_to_all(mirror_part, 'graph', split_axis=1, concat_axis=1, tiled=T...  7.74 us
    all_to_all x2, starting transfers between devices, on_device(): lax.all_to_all(outgoing, 'graph', split_axis=1, concat_axis=1, tiled=True)  6.71 us
    gather x3, local copies, waits for them, and re-layouts, on_device(): receivers = node_table[:, edge_recv]  6.52 us
    all_to_all x1, starting transfers between devices, on_device(): lax.all_to_all(counts_out, 'graph', split_axis=1, concat_axis=1, tiled=True)  6.32 us
  transfers between devices with their start and end apart: 9, of which 2 were waited for; matrix products, arithmetic and copies ran while one was open for 26% of the time, Pallas kernels for 0%

commit v1 on v0

--- a/solution.py
+++ b/solution.py
@@ -1,7 +1,16 @@
+import functools
+
 import jax
 import jax.numpy as jnp
 from jax import lax
+from jax.experimental import pallas as pl
+from jax.experimental.pallas import tpu as pltpu
 from jax.sharding import PartitionSpec as P
+
+BLOCK = 32
+BF = jnp.bfloat16
+F32 = jnp.float32
+MESH = pl.DeviceIdType.MESH
 
 
 def layer_norm(projected, gain_row):
@@ -132,6 +141,341 @@
     return (fine_state, coarse_state, edge_state)
 
 
+def mm(a, b):
+    return jnp.dot(a, b, preferred_element_type=F32)
+
+
+def silu(v):
+    half = 0.5 * v
+    return half + half * jnp.tanh(half)
+
+
+def kernel(
+    sizes,
+    idx_ref, fine_ref, coarse_ref, edge_ref,
+    ew1_ref, ew2_ref, nw1_ref, nw2_ref,
+    eb_ref, eg_ref, nb_ref, ng_ref,
+    fine_out, coarse_out, edge_out,
+    we, wn, state, outb, tab, sumb, ret, upd, gat_s, gat_r, sct,
+    own_sem, a_send, a_recv, f_send, f_recv, s_send, s_recv,
+    d_send, d_recv, x_send, x_recv, out_send, out_recv, ret_send, ret_recv,
+):
+    planes, share, coarse_total, owned, slots_edge, latent = sizes
+    group = lax.axis_index("group")
+    me = lax.axis_index("graph")
+    member = lax.axis_index("member")
+    x = member // 2
+    c = member % 2
+    across = (1 - x) * 2 + c
+    here = (group, me, member)
+    sibling = (group, me, x * 2 + 1 - c)
+    first = (group + c * (1 - 2 * group), me, member + (1 - c) * (across - member))
+    second = (group + (1 - c) * (1 - 2 * group), me, member + c * (across - member))
+    spot = lambda dev: dev[0] * 2 + dev[2] // 2
+    mine, spot_f, spot_s = spot(here), spot(first), spot(second)
+    spot_d = 3 - mine
+    peers = [(d, lax.rem(me + d, planes)) for d in range(1, planes)]
+
+    def remote(src, dst, send, recv, dev):
+        copy = pltpu.make_async_remote_copy(
+            src_ref=src, dst_ref=dst, send_sem=send, recv_sem=recv,
+            device_id=dev, device_id_type=MESH,
+        )
+        copy.start()
+
+    def wait(ref, sem):
+        pltpu.make_async_copy(ref, ref, sem).wait()
+
+    barrier = pltpu.get_barrier_semaphore()
+    partners = [(group, q, member) for _, q in peers] + [first, second, sibling]
+    for dev in partners:
+        pl.semaphore_signal(barrier, inc=1, device_id=dev, device_id_type=MESH)
+
+    re1, re2, rn1, rn2 = (r.shape[3] for r in (ew1_ref, ew2_ref, nw1_ref, nw2_ref))
+    edge_parts = [(ew1_ref, 0, re1), (ew2_ref, re1, re2)]
+    node_parts = [(nw1_ref, 0, rn1), (nw2_ref, rn1, rn2)]
+    groups = [(we, 0, edge_parts), (wn, 0, node_parts), (we, 1, edge_parts), (wn, 1, node_parts)]
+
+    for k, (buf, layer, parts) in enumerate(groups):
+        for src, at, rows in parts:
+            pltpu.make_async_copy(
+                src.at[layer], buf.at[layer, me, :, :, pl.ds(at, rows)], own_sem.at[k]
+            ).start()
+
+    def start_a(k):
+        buf, layer, parts = groups[k]
+        for d, q in peers:
+            for src, at, rows in parts:
+                remote(
+                    src.at[layer, c, mine],
+                    buf.at[layer, me, c, mine, pl.ds(at, rows)],
+                    a_send.at[k, d - 1], a_recv.at[k, planes - d - 1],
+                    (group, q, member),
+                )
+
+    def step_a(k):
+        buf, layer, _ = groups[k]
+        for d, q in peers:
+            piece = buf.at[layer, q, c, mine]
+            wait(piece, a_recv.at[k, d - 1])
+            remote(piece, piece, f_send.at[k, d - 1], f_recv.at[k, d - 1], first)
+            remote(piece, piece, s_send.at[k, d - 1], s_recv.at[k, d - 1], second)
+
+    def step_c(k):
+        buf, layer, _ = groups[k]
+        for d, q in peers:
+            piece = buf.at[layer, q, c, spot_f]
+            wait(piece, f_recv.at[k, d - 1])
+            remote(piece, piece, d_send.at[k, d - 1], d_recv.at[k, d - 1], second)
+
+    def step_d(k):
+        buf, layer, _ = groups[k]
+        for d, q in peers:
+            wait(buf.at[layer, q, c, spot_s], s_recv.at[k, d - 1])
+            wait(buf.at[layer, q, c, spot_d], d_recv.at[k, d - 1])
+            block = buf.at[layer, q, c]
+            remote(block, block, x_send.at[k, d - 1], x_recv.at[k, d - 1], sibling)
+
+    def step_x(k):
+        buf, layer, _ = groups[k]
+        for d, q in peers:
+            wait(buf.at[layer, q, 1 - c], x_recv.at[k, d - 1])
+        wait(buf.at[layer, me], own_sem.at[k])
+
+    def onehot(values, axis, size):
+        shape = (size, values.shape[1]) if axis == 0 else (values.shape[0], size)
+        spots = lax.broadcasted_iota(jnp.int32, shape, axis).astype(F32)
+        return jnp.where(values == spots, 1.0, 0.0).astype(BF)
+
+    table_rows = planes * BLOCK + owned
+    state_rows = owned + BLOCK
+    idx = idx_ref[...]
+    cols = jnp.transpose(idx)
+    row = lax.broadcasted_iota(jnp.int32, (BLOCK, coarse_total), 0)
+    col = lax.broadcasted_iota(jnp.int32, (BLOCK, coarse_total), 1)
+    pick = jnp.where((row < share) & (col == me * share + row), 1.0, 0.0).astype(BF)
+    state[pl.ds(0, owned)] = fine_ref[...]
+    state[pl.ds(owned, BLOCK)] = mm(pick, coarse_ref[...]).astype(BF)
+    sel = onehot(cols[: planes * BLOCK, 2:3], 1, state_rows)
+    sel_t = onehot(idx[2:3, : planes * BLOCK], 0, state_rows)
+
+    def make_blocks(step):
+        outb[step] = mm(sel, state[...]).astype(BF).reshape(planes, BLOCK, latent)
+        tab[step, me] = outb[step, me]
+
+    def send_blocks(step):
+        for d, q in peers:
+            remote(
+                outb.at[step, q], tab.at[step, me],
+                out_send.at[step, d - 1], out_recv.at[step, planes - d - 1],
+                (group, q, member),
+            )
+
+    def wait_blocks(step):
+        for d, q in peers:
+            wait(tab.at[step, q], out_recv.at[step, d - 1])
+
+    make_blocks(0)
+    pl.semaphore_wait(barrier, len(partners))
+    send_blocks(0)
+    for k in range(4):
+        start_a(k)
+
+    gat_s[...] = onehot(cols[:, 0:1], 1, table_rows)
+    gat_r[...] = onehot(cols[:, 1:2], 1, table_rows)
+    sct[...] = onehot(idx[1:2, :], 0, table_rows)
+
+    def norm(y, gain):
+        centered = y - jnp.mean(y, axis=-1, keepdims=True)
+        variance = jnp.mean(centered * centered, axis=-1, keepdims=True)
+        return centered * lax.rsqrt(variance + 1e-05) * gain
+
+    half = slots_edge // 2
+
+    def edge_half(layer, part):
+        rows = pl.ds(part * half, half)
+        table = jnp.concatenate(
+            [tab[layer].reshape(planes * BLOCK, latent), state[pl.ds(0, owned)]], axis=0
+        )
+        prior = (edge_ref if layer == 0 else edge_out)[rows]
+        sender = mm(gat_s[rows], table).astype(BF)
+        receiver = mm(gat_r[rows], table).astype(BF)
+        inputs = jnp.concatenate([prior, sender, receiver], axis=1)
+        w1 = we[layer, :, :, :, pl.ds(0, re1)].reshape(3 * latent, latent)
+        w2 = we[layer, :, :, :, pl.ds(re1, re2)].reshape(latent, latent)
+        hidden = silu(mm(inputs, w1) + eb_ref[pl.ds(layer, 1)]).astype(BF)
+        update = norm(mm(hidden, w2), eg_ref[pl.ds(layer, 1)])
+        live = cols[part * half : (part + 1) * half, 1:2] >= 0.0
+        edge_out[rows] = (prior.astype(F32) + jnp.where(live, update, 0.0)).astype(BF)
+        upd[rows] = update.astype(BF)
+
+    def send_sums(layer):
+        sums = mm(sct[pl.ds(0, planes * BLOCK)], upd[...])
+        sumb[layer] = sums.astype(BF).reshape(planes, BLOCK, latent)
+        for d, q in peers:
+            remote(
+                sumb.at[layer, q], ret.at[layer, me],
+                ret_send.at[layer, d - 1], ret_recv.at[layer, planes - d - 1],
+                (group, q, member),
+            )
+        ret[layer, me] = sumb[layer, me]
+        return mm(sct[pl.ds(planes * BLOCK, owned)], upd[...])
+
+    def node(layer, own):
+        for d, q in peers:
+            wait(ret.at[layer, q], ret_recv.at[layer, d - 1])
+        back = mm(sel_t, ret[layer].reshape(planes * BLOCK, latent))
+        total = jnp.concatenate([own + back[:owned], back[owned:]], axis=0).astype(BF)
+        inputs = jnp.concatenate([state[...], total], axis=1)
+        w1 = wn[layer, :, :, :, pl.ds(0, rn1)].reshape(2 * latent, latent)
+        w2 = wn[layer, :, :, :, pl.ds(rn1, rn2)].reshape(latent, latent)
+        hidden = silu(mm(inputs, w1) + nb_ref[pl.ds(layer, 1)]).astype(BF)
+        change = norm(mm(hidden, w2), ng_ref[pl.ds(layer, 1)])
+        state[...] = (state[...].astype(F32) + change).astype(BF)
+
+    step_a(0)
+    step_c(0)
+    step_a(1)
+    step_d(0)
+    step_x(0)
+    wait_blocks(0)
+    step_c(1)
+    edge_half(0, 0)
+    step_a(2)
+    step_d(1)
+    edge_half(0, 1)
+    own = send_sums(0)
+    step_c(2)
+    step_a(3)
+    step_x(1)
+    node(0, own)
+    make_blocks(1)
+    send_blocks(1)
+    step_d(2)
+    step_c(3)
+    step_x(2)
+    wait_blocks(1)
+    edge_half(1, 0)
+    step_d(3)
+    edge_half(1, 1)
+    own = send_sums(1)
+    step_x(3)
+    node(1, own)
+    make_blocks(2)
+    send_blocks(2)
+    fine_out[...] = state[pl.ds(0, owned)]
+    row = lax.broadcasted_iota(jnp.int32, (coarse_total, planes * BLOCK), 0)
+    col = lax.broadcasted_iota(jnp.int32, (coarse_total, planes * BLOCK), 1)
+    place = row
+    for q in range(1, planes):
+        place = place + jnp.where(row >= q * share, BLOCK - share, 0)
+    unpick = jnp.where(place == col, 1.0, 0.0).astype(BF)
+    wait_blocks(2)
+    coarse_out[...] = mm(unpick, tab[2].reshape(planes * BLOCK, latent)).astype(BF)
+
+    for k, (buf, layer, _) in enumerate(groups):
+        for d, q in peers:
+            piece = buf.at[layer, q, c, mine]
+            for sem in (a_send, f_send, s_send, d_send):
+                wait(piece, sem.at[k, d - 1])
+            wait(buf.at[layer, q, c], x_send.at[k, d - 1])
+    for d, q in peers:
+        for step in range(3):
+            wait(outb.at[step, q], out_send.at[step, d - 1])
+        for layer in range(2):
+            wait(sumb.at[layer, q], ret_send.at[layer, d - 1])
+
+
+def on_device_kernel(
+    fine_nodes, coarse_nodes, edge_latents, edge_send, edge_recv, edge_count,
+    send_index, send_count, edge_w1, edge_w2, node_w1, node_w2,
+    edge_bias, edge_gain, node_bias, node_gain,
+):
+    planes = lax.axis_size("graph")
+    _, owned, latent = fine_nodes.shape
+    coarse_total = coarse_nodes.shape[1]
+    slots_edge = edge_latents.shape[1]
+    slots = send_index.shape[2]
+    share = coarse_total // planes
+    layers = edge_w1.shape[0]
+    base = coarse_total + owned
+    top = planes * BLOCK
+
+    def spread(local):
+        listed = local - base
+        return jnp.where(
+            local < coarse_total,
+            local // share * BLOCK + local % share,
+            jnp.where(
+                local < base,
+                local - coarse_total + top,
+                listed // slots * BLOCK + BLOCK - slots + listed % slots,
+            ),
+        )
+
+    live = jnp.arange(slots_edge, dtype=jnp.int32) < edge_count[0]
+    slot = jnp.arange(slots, dtype=jnp.int32)
+    listed = jnp.where(slot[None] < send_count[0][:, None], send_index[0], -1)
+    lead = jnp.arange(BLOCK - slots, dtype=jnp.int32)
+    lead = jnp.where(lead < share, owned + lead, -1)
+    target = jnp.concatenate(
+        [jnp.broadcast_to(lead[None], (planes, BLOCK - slots)), listed], axis=1
+    ).reshape(top)
+    idx = jnp.stack(
+        [
+            spread(edge_send),
+            jnp.where(live, spread(edge_recv), -1),
+            jnp.pad(target, (0, slots_edge - top), constant_values=-1),
+        ]
+    )
+    idx = jnp.pad(idx, ((0, 5), (0, 0))).astype(F32)
+
+    def cut(weight):
+        return weight.reshape(layers, 2, 4, weight.shape[1] // 8, latent)
+
+    weights = [cut(w) for w in (edge_w1, edge_w2, node_w1, node_w2)]
+    edge_rows = weights[0].shape[3] + weights[1].shape[3]
+    node_rows = weights[2].shape[3] + weights[3].shape[3]
+    sizes = (planes, share, coarse_total, owned, slots_edge, latent)
+    vmem = pl.BlockSpec(memory_space=pltpu.VMEM)
+    anywhere = pl.BlockSpec(memory_space=pl.ANY)
+    per_group = pltpu.SemaphoreType.DMA((2 * layers, planes - 1))
+    fine, coarse, edge = pl.pallas_call(
+        functools.partial(kernel, sizes),
+        out_shape=(
+            jax.ShapeDtypeStruct((owned, latent), BF),
+            jax.ShapeDtypeStruct((coarse_total, latent), BF),
+            jax.ShapeDtypeStruct((slots_edge, latent), BF),
+        ),
+        in_specs=[vmem] * 4 + [anywhere] * 4 + [vmem] * 4,
+        out_specs=(vmem, vmem, vmem),
+        scratch_shapes=[
+            pltpu.VMEM((layers, planes, 2, 4, edge_rows, latent), BF),
+            pltpu.VMEM((layers, planes, 2, 4, node_rows, latent), BF),
+            pltpu.VMEM((owned + BLOCK, latent), BF),
+            pltpu.VMEM((3, planes, BLOCK, latent), BF),
+            pltpu.VMEM((3, planes, BLOCK, latent), BF),
+            pltpu.VMEM((2, planes, BLOCK, latent), BF),
+            pltpu.VMEM((2, planes, BLOCK, latent), BF),
+            pltpu.VMEM((slots_edge, latent), BF),
+            pltpu.VMEM((slots_edge, top + owned), BF),
+            pltpu.VMEM((slots_edge, top + owned), BF),
+            pltpu.VMEM((top + owned, slots_edge), BF),
+            pltpu.SemaphoreType.DMA((2 * layers,)),
+        ]
+        + [per_group] * 10
+        + [pltpu.SemaphoreType.DMA((3, planes - 1))] * 2
+        + [pltpu.SemaphoreType.DMA((2, planes - 1))] * 2,
+        compiler_params=pltpu.CompilerParams(
+            collective_id=0, has_side_effects=True, vmem_limit_bytes=50 * 1024 * 1024
+        ),
+    )(
+        idx, fine_nodes[0], coarse_nodes[0], edge_latents[0], *weights,
+        edge_bias, edge_gain, node_bias, node_gain,
+    )
+    return fine[None], coarse[None], edge[None]
+
+
 def solution(mesh):
     placed = (
         P(("group", "member"), "graph", None),
@@ -151,8 +495,10 @@
         P(),
         P(),
     )
+    small = dict(mesh.shape) == {"group": 2, "graph": 4, "member": 4}
+    body = on_device_kernel if small else on_device
     return jax.shard_map(
-        on_device,
+        body,
         mesh=mesh,
         in_specs=placed,
         out_specs=(

time: 244 us -> 74.1 us (0.30)
  blocking collectives: 132 us -> 0 us
  Pallas kernels: 0 us -> 61.9 us
  local copies, waits for them, and re-layouts: 33.9 us -> 8.04 us
  starting transfers between devices: 20.9 us -> 0 us
  other arithmetic: 23.1 us -> 2.26 us
  between operations: 15.1 us -> 1.42 us
  matrix products: 11.7 us -> 0 us
  waiting for transfers between devices: 6.42 us -> 0 us
    all_gather x4 -> x0, blocking collectives: 85.9 us -> none  [project(): full_weight = lax.all_gather(weight, 'graph', axis=0, tiled=True)]
    pallas_call x0 -> x1, Pallas kernels: none -> 61.9 us  [on_device_kernel(): pl.pallas_call(functools.partial(kernel, sizes), out_shape=(jax.ShapeDtyp...]
    psum x2 -> x0, blocking collectives: 46.2 us -> none  [on_device(): coarse_sum = lax.psum(coarse_part, 'graph')]
    all_to_all x5 -> x0, starting transfers between devices: 20.8 us -> none  [the longest x2 7.74 us: on_device(): lax.all_to_all(mirror_part, 'graph', split_axis=1, concat_axis=1, tiled=T...]
    gather x9 -> x0, local copies, waits for them, and re-layouts: 19.4 us -> none  [the longest x3 6.52 us: on_device(): receivers = node_table[:, edge_recv]]
    scatter-add x4 -> x0, other arithmetic: 17.3 us -> none  [scatter_rows(): jax.ops.segment_sum(member_rows, indices, num_segments=count)]
    dot_general x4 -> x0, matrix products: 11.7 us -> none  [project(): return jnp.dot(inputs, full_weight, preferred_element_type=jnp.float32)]
    slice x15 -> x0, local copies, waits for them, and re-layouts: 5.65 us -> none  [the longest x1 2.09 us: on_device(): edge_w1[layer_idx]]
  transfers between devices with their start and end apart: 9 -> 0, of which waited for: 2 -> 0; matrix products, arithmetic and copies ran while one was open for 26% -> 0% of each run, Pallas kernels for 0% -> 0%
where the time goes in v1:
time: 74.1 us; the launch traced here: 73.7 us
  Pallas kernels  61.9 us (84%)
  local copies, waits for them, and re-layouts  8.04 us (11%)
  other arithmetic  2.26 us (3%)
  between operations  1.42 us (2%)
    pallas_call x1, Pallas kernels, on_device_kernel(): pl.pallas_call(functools.partial(kernel, sizes), out_shape=(jax.ShapeDtyp...  61.9 us
    unnamed x23, local copies, waits for them, and re-layouts  7.93 us

profile of v1, /device:TPU:0, one launch (start us, length us, event | category | flops | bytes accessed | tf_op | source)
XLA Modules:
  0.0 73.7 jit_solution(10170544747785831276)
XLA Ops:
  0.6 0.0 copy-start.5
  1.3 0.8 %bitcast_select_fusion = s32[4,8]{1,0:T(4,128)S(1)} fusion(s32[1,4,8]{2,1,0:T(4,128)} %param.22, s32[4]{0:T(128)} %bitcast.25), kind=kLoop, calls=%fused_computation.49 | loop fusion | flops 64 | bytes 272 | tf_op jit(solution)/shard_map/jit(_where)/select_n | solution.py:418
  2.1 0.1 pad_add_fusion.1
  2.2 0.1 reshape.29
  2.3 0.7 fusion.10
  3.0 0.7 fusion.2
  3.7 0.0 copy-start.6
  3.7 0.0 copy-start.7
  3.8 0.0 copy-start.8
  3.8 0.0 copy-start.9
  3.8 0.0 copy-done.5
  3.8 0.6 copy-done.6
  4.4 0.0 copy-done.7
  4.4 0.0 copy-done.8
  4.5 0.0 copy-done.9
  4.5 1.1 %copy-done = bf16[1,768,512]{2,1,0:T(8,128)(2,1)S(1)} copy-done((bf16[1,768,512]{2,1,0:T(8,128)(2,1)S(1)}, bf16[1,768,512]{2,1,0:T(8,128)(2,1)}, u32[]{:S(2)}) %copy-start) | copy-done | bytes 786456
  5.6 1.0 %copy-done.1 = bf16[2,256,512]{2,1,0:T(8,128)(2,1)S(1)} copy-done((bf16[2,256,512]{2,1,0:T(8,128)(2,1)S(1)}, bf16[2,256,512]{2,1,0:T(8,128)(2,1)}, u32[]{:S(2)}) %copy-start.1) | copy-done | bytes 524312
  6.6 0.9 %copy-done.2 = bf16[1,256,512]{2,1,0:T(8,128)(2,1)S(1)} copy-done((bf16[1,256,512]{2,1,0:T(8,128)(2,1)S(1)}, bf16[1,256,512]{2,1,0:T(8,128)(2,1)}, u32[]{:S(2)}) %copy-start.2) | copy-done | bytes 262168
  7.6 0.9 %copy-done.3 = bf16[2,128,512]{2,1,0:T(8,128)(2,1)S(1)} copy-done((bf16[2,128,512]{2,1,0:T(8,128)(2,1)S(1)}, bf16[2,128,512]{2,1,0:T(8,128)(2,1)}, u32[]{:S(2)}) %copy-start.3) | copy-done | bytes 262168
  8.5 0.9 %copy-done.4 = bf16[2,128,512]{2,1,0:T(8,128)(2,1)S(1)} copy-done((bf16[2,128,512]{2,1,0:T(8,128)(2,1)S(1)}, bf16[2,128,512]{2,1,0:T(8,128)(2,1)}, u32[]{:S(2)}) %copy-start.4) | copy-done | bytes 262168
  9.5 61.9 %shard_map.175 = (bf16[256,512]{1,0:T(8,128)(2,1)S(1)}, bf16[80,512]{1,0:T(8,128)(2,1)S(1)}, bf16[768,512]{1,0:T(8,128)(2,1)S(1)}) custom-call(f32[8,768]{1,0:T(8,128)S(1)} %pad_convert_fusion.idx_ref, bf16[256,512]{1,0:T(8,128)(2,1)S(1)} %bitcast.18, bf16[80,512]{1,0:T(8,128)(2,1)S(1)} %bitcast.22, bf16[768,512]{1,0:T(8,128)(2,1)S(1)} %bitcast.16, ...), custom_call_target="tpu_custom_call" | custom-call | tf_op jit(solution)/shard_map/pallas_call | solution.py:443
  71.5 0.7 copy.23
  72.2 0.6 copy.24
  72.8 0.9 %copy.25 = bf16[1,768,512]{2,1,0:T(8,128)(2,1)} copy(bf16[1,768,512]{2,1,0:T(8,128)(2,1)S(1)} %bitcast.15) | data formatting | bytes 1572864
  (13 shorter events, 0.1 us)
Async XLA Ops:
  0.6 3.2 %copy-start.5 = (bf16[1,80,512]{2,1,0:T(8,128)(2,1)S(1)}, bf16[1,80,512]{2,1,0:T(8,128)(2,1)}, u32[]{:S(2)}) copy-start(bf16[1,80,512]{2,1,0:T(8,128)(2,1)} %param.17) | copy-start | bytes 245764
  3.7 0.7 copy-start.6
  3.7 0.7 copy-start.7
  3.8 0.7 copy-start.8
  3.8 0.7 copy-start.9
  4.5 1.1 %copy-start = (bf16[1,768,512]{2,1,0:T(8,128)(2,1)S(1)}, bf16[1,768,512]{2,1,0:T(8,128)(2,1)}, u32[]{:S(2)}) copy-start(bf16[1,768,512]{2,1,0:T(8,128)(2,1)} %param.18) | copy-start | bytes 2359300
  5.6 1.0 %copy-start.1 = (bf16[2,256,512]{2,1,0:T(8,128)(2,1)S(1)}, bf16[2,256,512]{2,1,0:T(8,128)(2,1)}, u32[]{:S(2)}) copy-start(bf16[2,256,512]{2,1,0:T(8,128)(2,1)} %param.26) | copy-start | bytes 1572868
  6.6 0.9 %copy-start.2 = (bf16[1,256,512]{2,1,0:T(8,128)(2,1)S(1)}, bf16[1,256,512]{2,1,0:T(8,128)(2,1)}, u32[]{:S(2)}) copy-start(bf16[1,256,512]{2,1,0:T(8,128)(2,1)} %param.16) | copy-start | bytes 786436
  7.6 0.9 %copy-start.3 = (bf16[2,128,512]{2,1,0:T(8,128)(2,1)S(1)}, bf16[2,128,512]{2,1,0:T(8,128)(2,1)}, u32[]{:S(2)}) copy-start(bf16[2,128,512]{2,1,0:T(8,128)(2,1)} %param.25) | copy-start | bytes 786436
  8.5 0.9 %copy-start.4 = (bf16[2,128,512]{2,1,0:T(8,128)(2,1)S(1)}, bf16[2,128,512]{2,1,0:T(8,128)(2,1)}, u32[]{:S(2)}) copy-start(bf16[2,128,512]{2,1,0:T(8,128)(2,1)} %param.27) | copy-start | bytes 786436

commit v2 on v1

--- a/solution.py
+++ b/solution.py
@@ -152,12 +152,14 @@
 
 def kernel(
     sizes,
-    idx_ref, fine_ref, coarse_ref, edge_ref,
+    send_ref, recv_ref, count_ref, list_ref, used_ref,
+    fine_ref, coarse_ref, edge_ref,
     ew1_ref, ew2_ref, nw1_ref, nw2_ref,
-    eb_ref, eg_ref, nb_ref, ng_ref,
+    eb_hbm, eg_hbm, nb_hbm, ng_hbm,
     fine_out, coarse_out, edge_out,
-    we, wn, state, outb, tab, sumb, ret, upd, gat_s, gat_r, sct,
-    own_sem, a_send, a_recv, f_send, f_recv, s_send, s_recv,
+    we, wn, state, coarse_in, eb_ref, eg_ref, nb_ref, ng_ref,
+    outb, tab, sumb, ret, upd, gat_s, gat_r, sct,
+    in_sem, own_sem, a_send, a_recv, f_send, f_recv, s_send, s_recv,
     d_send, d_recv, x_send, x_recv, out_send, out_recv, ret_send, ret_recv,
 ):
     planes, share, coarse_total, owned, slots_edge, latent = sizes
@@ -171,10 +173,12 @@
     sibling = (group, me, x * 2 + 1 - c)
     first = (group + c * (1 - 2 * group), me, member + (1 - c) * (across - member))
     second = (group + (1 - c) * (1 - 2 * group), me, member + c * (across - member))
+    corner = (1 - group, me, across)
     spot = lambda dev: dev[0] * 2 + dev[2] // 2
     mine, spot_f, spot_s = spot(here), spot(first), spot(second)
     spot_d = 3 - mine
     peers = [(d, lax.rem(me + d, planes)) for d in range(1, planes)]
+    near = [me + 1 - 2 * (me % 2), 2 - me // 2, 3 - 3 * (me // 2)]
 
     def remote(src, dst, send, recv, dev):
         copy = pltpu.make_async_remote_copy(
@@ -187,9 +191,21 @@
         pltpu.make_async_copy(ref, ref, sem).wait()
 
     barrier = pltpu.get_barrier_semaphore()
-    partners = [(group, q, member) for _, q in peers] + [first, second, sibling]
+    partners = [(group, q, member) for _, q in peers] + [first, second, corner, sibling]
     for dev in partners:
         pl.semaphore_signal(barrier, inc=1, device_id=dev, device_id_type=MESH)
+
+    rows_in = [
+        (fine_ref.at[0], state.at[pl.ds(0, owned)]), (coarse_ref.at[0], coarse_in),
+        (edge_ref.at[0], edge_out),
+        (eb_hbm, eb_ref), (eg_hbm, eg_ref), (nb_hbm, nb_ref), (ng_hbm, ng_ref),
+    ]
+    for n, (src, dst) in enumerate(rows_in):
+        pltpu.make_async_copy(src, dst, in_sem.at[n]).start()
+
+    def wait_in(*which):
+        for n in which:
+            wait(rows_in[n][1], in_sem.at[n])
 
     re1, re2, rn1, rn2 = (r.shape[3] for r in (ew1_ref, ew2_ref, nw1_ref, nw2_ref))
     edge_parts = [(ew1_ref, 0, re1), (ew2_ref, re1, re2)]
@@ -204,42 +220,38 @@
 
     def start_a(k):
         buf, layer, parts = groups[k]
-        for d, q in peers:
+
+        for q in near:
             for src, at, rows in parts:
                 remote(
                     src.at[layer, c, mine],
                     buf.at[layer, me, c, mine, pl.ds(at, rows)],
-                    a_send.at[k, d - 1], a_recv.at[k, planes - d - 1],
-                    (group, q, member),
+                    a_send.at[k, q], a_recv.at[k, me], (group, q, member),
                 )
 
     def step_a(k):
         buf, layer, _ = groups[k]
-        for d, q in peers:
+        for q in near:
             piece = buf.at[layer, q, c, mine]
-            wait(piece, a_recv.at[k, d - 1])
-            remote(piece, piece, f_send.at[k, d - 1], f_recv.at[k, d - 1], first)
-            remote(piece, piece, s_send.at[k, d - 1], s_recv.at[k, d - 1], second)
-
-    def step_c(k):
-        buf, layer, _ = groups[k]
-        for d, q in peers:
-            piece = buf.at[layer, q, c, spot_f]
-            wait(piece, f_recv.at[k, d - 1])
-            remote(piece, piece, d_send.at[k, d - 1], d_recv.at[k, d - 1], second)
+            wait(piece, a_recv.at[k, q])
+
+            remote(piece, piece, f_send.at[k, q], f_recv.at[k, q], first)
+            remote(piece, piece, s_send.at[k, q], s_recv.at[k, q], second)
+            remote(piece, piece, d_send.at[k, q], d_recv.at[k, q], corner)
 
     def step_d(k):
         buf, layer, _ = groups[k]
-        for d, q in peers:
-            wait(buf.at[layer, q, c, spot_s], s_recv.at[k, d - 1])
-            wait(buf.at[layer, q, c, spot_d], d_recv.at[k, d - 1])
+        for q in near:
+            wait(buf.at[layer, q, c, spot_f], f_recv.at[k, q])
+            wait(buf.at[layer, q, c, spot_s], s_recv.at[k, q])
+            wait(buf.at[layer, q, c, spot_d], d_recv.at[k, q])
             block = buf.at[layer, q, c]
-            remote(block, block, x_send.at[k, d - 1], x_recv.at[k, d - 1], sibling)
+            remote(block, block, x_send.at[k, q], x_recv.at[k, q], sibling)
 
     def step_x(k):
         buf, layer, _ = groups[k]
-        for d, q in peers:
-            wait(buf.at[layer, q, 1 - c], x_recv.at[k, d - 1])
+        for q in near:
+            wait(buf.at[layer, q, 1 - c], x_recv.at[k, q])
         wait(buf.at[layer, me], own_sem.at[k])
 
     def onehot(values, axis, size):
@@ -249,41 +261,81 @@
 
     table_rows = planes * BLOCK + owned
     state_rows = owned + BLOCK
-    idx = idx_ref[...]
+    top = planes * BLOCK
+    slots = list_ref.shape[2]
+
+    def spread(local):
+        listed = local - coarse_total - owned
+        low, high = local, listed + BLOCK - slots
+        for q in range(1, planes):
+            low = low + jnp.where(local >= q * share, BLOCK - share, 0)
+            high = high + jnp.where(listed >= q * slots, BLOCK - slots, 0)
+        return jnp.where(
+            local < coarse_total, low,
+            jnp.where(listed < 0, local - coarse_total + top, high),
+        )
+
+    lane = lax.broadcasted_iota(jnp.int32, (1, slots_edge), 1)
+    target = jnp.full((1, slots_edge), -1, jnp.int32)
+    for q in range(planes):
+        own_lane = lane - q * BLOCK
+        target = jnp.where((own_lane >= 0) & (own_lane < share), owned + own_lane, target)
+        for slot in range(slots):
+            node_of = jnp.where(slot < used_ref[0, q], list_ref[0, q, slot], -1)
+            target = jnp.where(own_lane == BLOCK - slots + slot, node_of, target)
+    receivers = jnp.where(lane < count_ref[0], spread(recv_ref[...]), -1)
+    line = lax.broadcasted_iota(jnp.int32, (8, slots_edge), 0)
+    idx = jnp.where(
+        line == 0, spread(send_ref[...]),
+        jnp.where(line == 1, receivers, jnp.where(line == 2, target, -1)),
+    ).astype(F32)
     cols = jnp.transpose(idx)
+    row = lax.broadcasted_iota(jnp.int32, (top, coarse_total), 0)
+    col = lax.broadcasted_iota(jnp.int32, (top, coarse_total), 1)
+    place = col
+    for q in range(1, planes):
+        place = place + jnp.where(col >= q * share, BLOCK - share, 0)
+    pick = jnp.where(row == place, 1.0, 0.0).astype(BF)
     row = lax.broadcasted_iota(jnp.int32, (BLOCK, coarse_total), 0)
     col = lax.broadcasted_iota(jnp.int32, (BLOCK, coarse_total), 1)
-    pick = jnp.where((row < share) & (col == me * share + row), 1.0, 0.0).astype(BF)
-    state[pl.ds(0, owned)] = fine_ref[...]
-    state[pl.ds(owned, BLOCK)] = mm(pick, coarse_ref[...]).astype(BF)
+    pick_own = jnp.where((row < share) & (col == me * share + row), 1.0, 0.0).astype(BF)
+    wait_in(0, 1)
+    state[pl.ds(owned, BLOCK)] = mm(pick_own, coarse_in[...]).astype(BF)
+    early = BLOCK // 2
+    blocks = mm(pick, coarse_in[...]).astype(BF).reshape(planes, BLOCK, latent)
+    tab[0, :, pl.ds(0, early)] = blocks[:, :early]
     sel = onehot(cols[: planes * BLOCK, 2:3], 1, state_rows)
     sel_t = onehot(idx[2:3, : planes * BLOCK], 0, state_rows)
 
+    def part_of(step):
+        return pl.ds(early, BLOCK - early) if step == 0 else pl.ds(0, BLOCK)
+
     def make_blocks(step):
         outb[step] = mm(sel, state[...]).astype(BF).reshape(planes, BLOCK, latent)
-        tab[step, me] = outb[step, me]
+        tab[step, me, part_of(step)] = outb[step, me, part_of(step)]
 
     def send_blocks(step):
         for d, q in peers:
             remote(
-                outb.at[step, q], tab.at[step, me],
+                outb.at[step, q, part_of(step)], tab.at[step, me, part_of(step)],
                 out_send.at[step, d - 1], out_recv.at[step, planes - d - 1],
                 (group, q, member),
             )
 
     def wait_blocks(step):
         for d, q in peers:
-            wait(tab.at[step, q], out_recv.at[step, d - 1])
+            wait(tab.at[step, q, part_of(step)], out_recv.at[step, d - 1])
 
     make_blocks(0)
     pl.semaphore_wait(barrier, len(partners))
+    start_a(0)
     send_blocks(0)
-    for k in range(4):
-        start_a(k)
+    start_a(1)
 
     gat_s[...] = onehot(cols[:, 0:1], 1, table_rows)
     gat_r[...] = onehot(cols[:, 1:2], 1, table_rows)
     sct[...] = onehot(idx[1:2, :], 0, table_rows)
+    wait_in(2, 3, 4, 5, 6)
 
     def norm(y, gain):
         centered = y - jnp.mean(y, axis=-1, keepdims=True)
@@ -297,7 +349,7 @@
         table = jnp.concatenate(
             [tab[layer].reshape(planes * BLOCK, latent), state[pl.ds(0, owned)]], axis=0
         )
-        prior = (edge_ref if layer == 0 else edge_out)[rows]
+        prior = edge_out[rows]
         sender = mm(gat_s[rows], table).astype(BF)
         receiver = mm(gat_r[rows], table).astype(BF)
         inputs = jnp.concatenate([prior, sender, receiver], axis=1)
@@ -334,25 +386,23 @@
         state[...] = (state[...].astype(F32) + change).astype(BF)
 
     step_a(0)
-    step_c(0)
     step_a(1)
     step_d(0)
+    start_a(2)
     step_x(0)
     wait_blocks(0)
-    step_c(1)
     edge_half(0, 0)
     step_a(2)
     step_d(1)
     edge_half(0, 1)
     own = send_sums(0)
-    step_c(2)
-    step_a(3)
+    start_a(3)
     step_x(1)
     node(0, own)
     make_blocks(1)
     send_blocks(1)
+    step_a(3)
     step_d(2)
-    step_c(3)
     step_x(2)
     wait_blocks(1)
     edge_half(1, 0)
@@ -364,26 +414,26 @@
     make_blocks(2)
     send_blocks(2)
     fine_out[...] = state[pl.ds(0, owned)]
-    row = lax.broadcasted_iota(jnp.int32, (coarse_total, planes * BLOCK), 0)
-    col = lax.broadcasted_iota(jnp.int32, (coarse_total, planes * BLOCK), 1)
+    row = lax.broadcasted_iota(jnp.int32, (coarse_total, top), 0)
+    col = lax.broadcasted_iota(jnp.int32, (coarse_total, top), 1)
     place = row
     for q in range(1, planes):
         place = place + jnp.where(row >= q * share, BLOCK - share, 0)
     unpick = jnp.where(place == col, 1.0, 0.0).astype(BF)
-    wait_blocks(2)
-    coarse_out[...] = mm(unpick, tab[2].reshape(planes * BLOCK, latent)).astype(BF)
-
     for k, (buf, layer, _) in enumerate(groups):
-        for d, q in peers:
+        for q in near:
             piece = buf.at[layer, q, c, mine]
-            for sem in (a_send, f_send, s_send, d_send):
-                wait(piece, sem.at[k, d - 1])
-            wait(buf.at[layer, q, c], x_send.at[k, d - 1])
+            wait(piece, a_send.at[k, q])
+            for sem in (f_send, s_send, d_send):
+                wait(piece, sem.at[k, q])
+            wait(buf.at[layer, q, c], x_send.at[k, q])
     for d, q in peers:
         for step in range(3):
-            wait(outb.at[step, q], out_send.at[step, d - 1])
+            wait(outb.at[step, q, part_of(step)], out_send.at[step, d - 1])
         for layer in range(2):
             wait(sumb.at[layer, q], ret_send.at[layer, d - 1])
+    wait_blocks(2)
+    coarse_out[...] = mm(unpick, tab[2].reshape(top, latent)).astype(BF)
 
 
 def on_device_kernel(
@@ -395,40 +445,9 @@
     _, owned, latent = fine_nodes.shape
     coarse_total = coarse_nodes.shape[1]
     slots_edge = edge_latents.shape[1]
-    slots = send_index.shape[2]
     share = coarse_total // planes
     layers = edge_w1.shape[0]
-    base = coarse_total + owned
     top = planes * BLOCK
-
-    def spread(local):
-        listed = local - base
-        return jnp.where(
-            local < coarse_total,
-            local // share * BLOCK + local % share,
-            jnp.where(
-                local < base,
-                local - coarse_total + top,
-                listed // slots * BLOCK + BLOCK - slots + listed % slots,
-            ),
-        )
-
-    live = jnp.arange(slots_edge, dtype=jnp.int32) < edge_count[0]
-    slot = jnp.arange(slots, dtype=jnp.int32)
-    listed = jnp.where(slot[None] < send_count[0][:, None], send_index[0], -1)
-    lead = jnp.arange(BLOCK - slots, dtype=jnp.int32)
-    lead = jnp.where(lead < share, owned + lead, -1)
-    target = jnp.concatenate(
-        [jnp.broadcast_to(lead[None], (planes, BLOCK - slots)), listed], axis=1
-    ).reshape(top)
-    idx = jnp.stack(
-        [
-            spread(edge_send),
-            jnp.where(live, spread(edge_recv), -1),
-            jnp.pad(target, (0, slots_edge - top), constant_values=-1),
-        ]
-    )
-    idx = jnp.pad(idx, ((0, 5), (0, 0))).astype(F32)
 
     def cut(weight):
         return weight.reshape(layers, 2, 4, weight.shape[1] // 8, latent)
@@ -438,8 +457,9 @@
     node_rows = weights[2].shape[3] + weights[3].shape[3]
     sizes = (planes, share, coarse_total, owned, slots_edge, latent)
     vmem = pl.BlockSpec(memory_space=pltpu.VMEM)
-    anywhere = pl.BlockSpec(memory_space=pl.ANY)
-    per_group = pltpu.SemaphoreType.DMA((2 * layers, planes - 1))
+    smem = pl.BlockSpec(memory_space=pltpu.SMEM)
+    hbm = pl.BlockSpec(memory_space=pltpu.HBM)
+    per_group = pltpu.SemaphoreType.DMA((2 * layers, planes))
     fine, coarse, edge = pl.pallas_call(
         functools.partial(kernel, sizes),
         out_shape=(
@@ -447,12 +467,16 @@
             jax.ShapeDtypeStruct((coarse_total, latent), BF),
             jax.ShapeDtypeStruct((slots_edge, latent), BF),
         ),
-        in_specs=[vmem] * 4 + [anywhere] * 4 + [vmem] * 4,
+        in_specs=[vmem] * 2 + [smem] * 3 + [hbm] * 11,
         out_specs=(vmem, vmem, vmem),
         scratch_shapes=[
             pltpu.VMEM((layers, planes, 2, 4, edge_rows, latent), BF),
             pltpu.VMEM((layers, planes, 2, 4, node_rows, latent), BF),
             pltpu.VMEM((owned + BLOCK, latent), BF),
+            pltpu.VMEM((coarse_total, latent), BF),
+        ]
+        + [pltpu.VMEM((layers, latent), F32)] * 4
+        + [
             pltpu.VMEM((3, planes, BLOCK, latent), BF),
             pltpu.VMEM((3, planes, BLOCK, latent), BF),
             pltpu.VMEM((2, planes, BLOCK, latent), BF),
@@ -461,16 +485,18 @@
             pltpu.VMEM((slots_edge, top + owned), BF),
             pltpu.VMEM((slots_edge, top + owned), BF),
             pltpu.VMEM((top + owned, slots_edge), BF),
-            pltpu.SemaphoreType.DMA((2 * layers,)),
+            pltpu.SemaphoreType.DMA((7,)),
         ]
+        + [pltpu.SemaphoreType.DMA((2 * layers,))]
         + [per_group] * 10
         + [pltpu.SemaphoreType.DMA((3, planes - 1))] * 2
         + [pltpu.SemaphoreType.DMA((2, planes - 1))] * 2,
         compiler_params=pltpu.CompilerParams(
-            collective_id=0, has_side_effects=True, vmem_limit_bytes=50 * 1024 * 1024
+            collective_id=0, has_side_effects=True, vmem_limit_bytes=62 * 1024 * 1024
         ),
     )(
-        idx, fine_nodes[0], coarse_nodes[0], edge_latents[0], *weights,
+        edge_send[None], edge_recv[None], edge_count, send_index, send_count,
+        fine_nodes, coarse_nodes, edge_latents, *weights,
         edge_bias, edge_gain, node_bias, node_gain,
     )
     return fine[None], coarse[None], edge[None]

time: 74.1 us -> 68.1 us (0.919)
  other arithmetic: 2.26 us -> 0 us
  local copies, waits for them, and re-layouts: 8.04 us -> 6.24 us
  Pallas kernels: 61.9 us -> 60.3 us
    unnamed x23 -> x9, local copies, waits for them, and re-layouts: 7.93 us -> 5.08 us
    select_n x4 -> x0, other arithmetic: 2.17 us -> none  [the longest x1 0.76 us: on_device_kernel(): listed = jnp.where(slot[None] < send_count[0][:, None], send_index[0], -1)]
    pallas_call x1, Pallas kernels: 61.9 us -> 60.3 us  [on_device_kernel(): pl.pallas_call(functools.partial(kernel, sizes), out_shape=(jax.ShapeDtyp...]
    broadcast_in_dim x0 -> x2, local copies, waits for them, and re-layouts: none -> 1.16 us  [the longest x1 0.58 us: on_device_kernel(): edge_recv[None]]
where the time goes in v2:
time: 68.1 us; the launch traced here: 67.9 us
  Pallas kernels  60.3 us (89%)
  local copies, waits for them, and re-layouts  6.24 us (9%)
  between operations  1.31 us (2%)
    pallas_call x1, Pallas kernels, on_device_kernel(): pl.pallas_call(functools.partial(kernel, sizes), out_shape=(jax.ShapeDtyp...  60.3 us
    unnamed x9, local copies, waits for them, and re-layouts  5.08 us

profile of v2, /device:TPU:0, one launch (start us, length us, event | category | flops | bytes accessed | tf_op | source)
XLA Modules:
  0.0 67.9 jit_solution(385654824452583643)
XLA Ops:
  1.3 0.0 copy-start.1
  1.3 0.0 copy-start.2
  1.3 0.7 copy-done.1
  2.0 0.6 broadcast_in_dim.15.send_ref
  2.5 0.0 copy-done.2
  2.5 0.6 broadcast_in_dim.16.recv_ref
  3.1 60.3 %shard_map.175 = (bf16[256,512]{1,0:T(8,128)(2,1)}, bf16[80,512]{1,0:T(8,128)(2,1)}, bf16[768,512]{1,0:T(8,128)(2,1)}) custom-call(s32[1,768]{1,0:T(1,128)} %broadcast_in_dim.15.send_ref, s32[1,768]{1,0:T(1,128)} %broadcast_in_dim.16.recv_ref, s32[1]{0:T(128)S(6)} %copy.22.count_ref, s32[1,4,8]{2,1,0:T(4,128)} %list_ref.1, s32[1,4]{1,0:T(1,128)} %used_ref.1, ...), custom_call_target="tpu_custom_call" | custom-call | tf_op jit(solution)/shard_map/pallas_call | solution.py:463
  63.4 0.0 copy-start
  63.4 1.7 %copy.23 = bf16[1,256,512]{2,1,0:T(8,128)(2,1)} copy(bf16[1,256,512]{2,1,0:T(8,128)(2,1)} %bitcast.10) | data formatting | bytes 524288
  65.2 0.0 copy-done
  65.2 0.6 copy.24
  65.8 2.1 %copy.25 = bf16[1,768,512]{2,1,0:T(8,128)(2,1)} copy(bf16[1,768,512]{2,1,0:T(8,128)(2,1)} %bitcast.7) | data formatting | bytes 1572864
Async XLA Ops:
  1.3 0.7 %copy-start.1 = (s32[768]{0:T(1024)S(1)}, s32[768]{0:T(1024)}, u32[]{:S(2)}) copy-start(s32[768]{0:T(1024)} %param.19) | copy-start | bytes 9220
  1.3 1.3 %copy-start.2 = (s32[768]{0:T(1024)S(1)}, s32[768]{0:T(1024)}, u32[]{:S(2)}) copy-start(s32[768]{0:T(1024)} %param.20) | copy-start | bytes 9220
  63.4 1.7 %copy-start = (bf16[80,512]{1,0:T(8,128)(2,1)S(1)}, bf16[80,512]{1,0:T(8,128)(2,1)}, u32[]{:S(2)}) copy-start(bf16[80,512]{1,0:T(8,128)(2,1)} %get-tuple-element.7) | copy-start | bytes 245764
